TPU v7x, 32 devices: a whole 2x2x4 slice. The times are simulated.
32 devices in a mesh: groups: 2 (over x), sx: 8 (over z, y), sy: 2 (over core).
Axes of the slice: x: 2, y: 2, z: 4, core: 2. Of those that a mesh axis runs over, the one named last changes fastest.
Arguments:
- feature: bfloat16 [32, 64, 32, 128], P(('groups', 'sx'), 'sy'), parts along dimension 0, may hold values from -6 to 6
- weight_upper: bfloat16 [6912, 128], P('groups'), parts along dimension 0, may hold values from -0.109375 to 0.109375
- down_weight_matrix: bfloat16 [2048, 256], P('groups'), parts along dimension 0, may hold values from -0.1875 to 0.1875
- weight_lower: bfloat16 [13824, 256], P('groups'), parts along dimension 0, may hold values from -0.078125 to 0.078125
- cotangent: bfloat16 [16, 32, 16, 256], P(('groups', 'sx'), 'sy'), parts along dimension 0, may hold values from -6 to 6
Outputs:
- bottleneck: bfloat16 [16, 32, 16, 256], P(('groups', 'sx'), 'sy'), parts along dimension 0
- grad_feature: bfloat16 [32, 64, 32, 128], P(('groups', 'sx'), 'sy'), parts along dimension 0
- grad_upper: float32 [6912, 128], P(('groups', 'sx', 'sy')), parts along dimension 0
- down_weight_gradient: float32 [2048, 256], P(('groups', 'sx', 'sy')), parts along dimension 0
- grad_lower: float32 [13824, 256], P(('groups', 'sx', 'sy')), parts along dimension 0
There are 2 independent parts, one for each index of `groups`. A program takes and returns all parts, laid end to end along the dimension named above; each array names one. Nothing has to cross between parts.
All inputs are finite; a program needn't handle non-finite values.
Results may differ from a plain program's by a relative error of at most 0.006.
Values may be sent and summed in bfloat16 or wider, within the bound.
A program may use at most 128 MiB of HBM per device.

v0:
```python
import jax
import jax.numpy as jnp
from jax import lax
from jax.sharding import PartitionSpec as P


def extended(block, sides, width):
    for axis, dim in sides:
        count = lax.axis_size(axis)
        forward = [(i, i + 1) for i in range(count - 1)]
        backward = [(target, source) for source, target in forward]
        low = lax.ppermute(
            lax.slice_in_dim(block, block.shape[dim] - width, None, axis=dim), axis, forward
        )
        high = lax.ppermute(lax.slice_in_dim(block, 0, width, axis=dim), axis, backward)
        block = jnp.concatenate([low, block, high], axis=dim)
    return block


def activate(preact):
    return preact * jax.nn.sigmoid(preact)


def slope(preact):
    sigmoid_value = jax.nn.sigmoid(preact)
    return sigmoid_value * (1.0 + preact * (1.0 - sigmoid_value))


def pad_depth(field):
    return jnp.pad(field, ((0, 0), (0, 0), (1, 1), (0, 0)))


def pad_upper(field):
    spread = extended(field, (("sx", 0), ("sy", 1)), 1)
    return pad_depth(spread)


def pad_lower(field):
    spread = extended(field, (("sx", 0), ("sy", 1)), 1)
    return pad_depth(spread)


def correlate(left, right, layout, strides, padding, left_dilation, right_dilation):
    return lax.conv_general_dilated(
        left,
        right,
        strides,
        padding,
        lhs_dilation=left_dilation,
        rhs_dilation=right_dilation,
        dimension_numbers=layout,
        preferred_element_type=jnp.float32,
    )


def convolve(padded, weight_collection):
    in_width = padded.shape[3]
    out_width = weight_collection.shape[1]
    kernel = weight_collection.reshape(in_width, 3, 3, 3, out_width)
    summed = correlate(
        padded[None],
        kernel,
        ("NDHWC", "IDHWO", "NDHWC"),
        (1, 1, 1),
        ((0, 0), (0, 0), (0, 0)),
        (1, 1, 1),
        (1, 1, 1),
    )
    return summed[0]


def convolve_back(padded, weight_collection):
    in_width = weight_collection.shape[0] // 27
    out_width = weight_collection.shape[1]
    kernel = weight_collection.reshape(in_width, 3, 3, 3, out_width)[:, ::-1, ::-1, ::-1, :]
    summed = correlate(
        padded[None],
        kernel,
        ("NDHWC", "ODHWI", "NDHWC"),
        (1, 1, 1),
        ((0, 0), (0, 0), (0, 0)),
        (1, 1, 1),
        (1, 1, 1),
    )
    return summed[0]


def kernel_grad(padded, grads):
    in_width = padded.shape[3]
    out_width = grads.shape[3]
    summed = correlate(
        padded[None],
        grads[..., None],
        ("CDHWN", "DHWOI", "NDHWC"),
        (1, 1, 1),
        ((0, 0), (0, 0), (0, 0)),
        (1, 1, 1),
        (1, 1, 1),
    )
    return summed.reshape(in_width * 27, out_width)


def strided_reduce(finer_feature, weight_collection):
    in_width = finer_feature.shape[3]
    out_width = weight_collection.shape[1]
    kernel = weight_collection.reshape(in_width, 2, 2, 2, out_width)
    summed = correlate(
        finer_feature[None],
        kernel,
        ("NDHWC", "IDHWO", "NDHWC"),
        (2, 2, 2),
        ((0, 0), (0, 0), (0, 0)),
        (1, 1, 1),
        (1, 1, 1),
    )
    return summed[0]


def strided_reduce_adjoint(finer_feature, coarse_gradient, weight_collection):
    in_width = finer_feature.shape[3]
    out_width = weight_collection.shape[1]
    kernel = weight_collection.reshape(in_width, 2, 2, 2, out_width)[:, ::-1, ::-1, ::-1, :]
    data_grad = correlate(
        coarse_gradient[None],
        kernel,
        ("NDHWC", "ODHWI", "NDHWC"),
        (1, 1, 1),
        ((1, 1), (1, 1), (1, 1)),
        (2, 2, 2),
        (1, 1, 1),
    )[0]
    weight_grad = correlate(
        finer_feature[None],
        coarse_gradient[..., None],
        ("CDHWN", "DHWOI", "NDHWC"),
        (1, 1, 1),
        ((0, 0), (0, 0), (0, 0)),
        (1, 1, 1),
        (2, 2, 2),
    )
    return (data_grad, weight_grad.reshape(in_width * 8, out_width))


def whole_volume(rows, extent):
    slabs_x = lax.axis_size("sx")
    slabs_y = lax.axis_size("sy")
    width = rows.shape[1]
    blocks = rows.reshape(slabs_x, slabs_y, extent[0], extent[1], extent[2], width)
    return blocks.transpose(0, 2, 1, 3, 4, 5).reshape(
        slabs_x * extent[0], slabs_y * extent[1], extent[2], width
    )


def body(feature, weight_upper, down_weight_matrix, weight_lower, cotangent):
    extent_lower = cotangent.shape[:3]
    lower_width = cotangent.shape[3]
    lower_voxels = extent_lower[0] * extent_lower[1] * extent_lower[2]
    cotangent_rows = lax.all_gather(
        cotangent.reshape(lower_voxels, lower_width), ("sx", "sy"), axis=0, tiled=True
    )
    padded_feature = pad_upper(feature)
    pre_upper = convolve(padded_feature, weight_upper)
    upper_hidden_feature = activate(pre_upper).astype(jnp.bfloat16)
    lower_preactivation = strided_reduce(upper_hidden_feature, down_weight_matrix)
    hidden_lower = activate(lower_preactivation).astype(jnp.bfloat16)
    padded_lower = pad_lower(hidden_lower)
    bottleneck = convolve(padded_lower, weight_lower).astype(jnp.bfloat16)
    owned_rows = lax.all_to_all(
        hidden_lower.reshape(lower_voxels, lower_width),
        ("sx", "sy"),
        split_axis=1,
        concat_axis=0,
        tiled=True,
    )
    grad_hidden_lower = convolve_back(pad_lower(cotangent), weight_lower)
    lower_preact_gradient = (grad_hidden_lower * slope(lower_preactivation)).astype(jnp.bfloat16)
    owned_volume = whole_volume(owned_rows, extent_lower)
    whole_cotangent = whole_volume(cotangent_rows, extent_lower)
    padded_owned = jnp.pad(owned_volume, ((1, 1), (1, 1), (1, 1), (0, 0)))
    lower_rows = kernel_grad(padded_owned, whole_cotangent)
    upper_hidden_gradient, downward_products = strided_reduce_adjoint(
        upper_hidden_feature, lower_preact_gradient, down_weight_matrix
    )
    grad_pre_upper = (upper_hidden_gradient * slope(pre_upper)).astype(jnp.bfloat16)
    upper_terms = kernel_grad(padded_feature, grad_pre_upper)
    grad_feature = convolve_back(pad_upper(grad_pre_upper), weight_upper).astype(jnp.bfloat16)
    down_rows, upper_rows = (
        lax.psum_scatter(downward_products, ("sx", "sy"), scatter_dimension=0, tiled=True),
        lax.psum_scatter(upper_terms, ("sx", "sy"), scatter_dimension=0, tiled=True),
    )
    return (bottleneck, grad_feature, upper_rows, down_rows, lower_rows)


def solution(mesh):
    placed = (
        P(("groups", "sx"), "sy", None, None),
        P("groups", None),
        P("groups", None),
        P("groups", None),
        P(("groups", "sx"), "sy", None, None),
    )
    return jax.shard_map(
        body,
        mesh=mesh,
        in_specs=placed,
        out_specs=(
            P(("groups", "sx"), "sy", None, None),
            P(("groups", "sx"), "sy", None, None),
            P(("groups", "sx", "sy"), None),
            P(("groups", "sx", "sy"), None),
            P(("groups", "sx", "sy"), None),
        ),
        check_vma=False,
    )
```

profile of v0, /device:TPU:0, one launch (start us, length us, event | category | flops | bytes accessed | tf_op | source)
XLA Modules:
  0.0 217.2 jit_solution(10850845552631957821)
XLA Ops:
  7.2 4.9 %collective-permute-start.8 = (bf16[1,16,16,256]{3,2,1,0:T(8,128)(2,1)}, bf16[1,16,16,256]{3,2,1,0:T(8,128)(2,1)S(1)}, u32[]{:S(2)}, u32[]{:S(2)}) collective-permute-start(bf16[1,16,16,256]{3,2,1,0:T(8,128)(2,1)} %param.9), channel_id=1, source_target_pairs={{0,2},{2,4},{4,6},{6,8},{8,10},{10,12},{12,14},{1,3},{3,5},{5,7},{... | collective-permute-start | bytes 393224 | tf_op jit(solution)/shard_map/ppermute | solution.py:12
  12.1 1.3 collective-permute-start.9
  13.4 1.9 fusion.151
  15.3 4.5 %collective-permute-start = (bf16[1,32,32,128]{3,2,1,0:T(8,128)(2,1)}, bf16[1,32,32,128]{3,2,1,0:T(8,128)(2,1)S(1)}, u32[]{:S(2)}, u32[]{:S(2)}) collective-permute-start(bf16[1,32,32,128]{3,2,1,0:T(8,128)(2,1)} %get-tuple-element.36), channel_id=1, source_target_pairs={{0,2},{2,4},{4,6},{6,8},{8,10},{10,12},{12,14},{1,3},{3,5},{5,7},{... | collective-permute-start | bytes 786440 | tf_op jit(solution)/shard_map/ppermute | solution.py:12
  19.9 0.6 fusion.152
  20.5 1.3 collective-permute-start.11
  21.8 4.2 %collective-permute-start.10 = (bf16[3,1,16,256]{3,2,1,0:T(8,128)(2,1)S(1)}, bf16[3,1,16,256]{3,2,1,0:T(8,128)(2,1)}, u32[]{:S(2)}, u32[]{:S(2)}) collective-permute-start(bf16[3,1,16,256]{3,2,1,0:T(8,128)(2,1)S(1)} %get-tuple-element.37), channel_id=1, source_target_pairs={{0,1},{2,3},{4,5},{6,7},{8,9},{10,11},{12,13},{14,15},{16,17},{18,... | collective-permute-start | bytes 73736 | tf_op jit(solution)/shard_map/ppermute | solution.py:12
  26.0 1.3 collective-permute-start.1
  27.4 8.9 %reshape.211 = bf16[256,3,3,3,256]{4,3,2,1,0:T(4,128)(2,1)} reshape(bf16[6912,256]{1,0:T(8,128)(2,1)} %param.8) | data formatting | bytes 7077888 | tf_op jit(solution)/shard_map/reshape | solution.py:59
  36.5 1.0 copy-done.8
  37.5 0.4 reshape.209
  37.9 1.2 fusion.96
  39.8 0.7 copy-done.3
  40.6 1.0 constant_dynamic-update-slice_fusion
  41.6 1.3 collective-permute-start.3
  42.9 3.6 %collective-permute-start.2 = (bf16[4,1,32,128]{3,2,1,0:T(8,128)(2,1)S(1)}, bf16[4,1,32,128]{3,2,1,0:T(8,128)(2,1)S(1)}, u32[]{:S(2)}, u32[]{:S(2)}) collective-permute-start(bf16[4,1,32,128]{3,2,1,0:T(8,128)(2,1)S(1)} %get-tuple-element.31), channel_id=1, source_target_pairs={{0,1},{2,3},{4,5},{6,7},{8,9},{10,11},{12,13},{14,15},{16,17},{18,... | collective-permute-start | bytes 98312 | tf_op jit(solution)/shard_map/ppermute | solution.py:12
  46.5 3.9 %fusion.56 = f32[1,16,8,3,256]{4,2,3,1,0:T(8,128)S(1)} fusion(bf16[256,3,3,3,256]{4,3,2,1,0:T(4,128)(2,1)} %reshape.211, bf16[3,18,1,7,2,256]{5,3,4,1,0,2:T(8,128)(2,1)S(1)} %slice.70, bf16[3,18,1,8,3,256]{5,3,4,1,0,2:T(8,128)(2,1)S(1)} %copy.166, pred[8,3]{0,1:T(4,128)(4,1)S(1)} %copy-done.11), kind=kOutput, calls=%fused_computation.61 | convolution fusion | flops 1362370560 | bytes 4982808 | tf_op jit(solution)/shard_map/conv_general_dilated | solution.py:44
  50.6 1.8 fusion.147
  52.5 0.5 copy.206
  52.9 0.5 pad.23.clone
  54.1 5.3 %broadcast_select_fusion = (bf16[2,32,8,5,128]{4,2,3,1,0:T(8,128)(2,1)S(1)}, bf16[2,32,8,5,128]{4,2,3,1,0:T(8,128)(2,1)S(1)}, f32[2,32,8,5,128]{4,2,3,1,0:T(8,128)S(1)}) fusion(pred[8,5]{0,1:T(8,128)(4,1)S(1)} %copy-done.13, bf16[128,3,3,3,128]{4,3,2,1,0:T(4,128)(2,1)S(1)} %reshape.209, bf16[4,34,1,7,2,128]{5,3,4,1,0,2:T(8,128)(2,1)S(1)} %slice.63, ...), kind=kOutput, calls=%fused_computation.114 | convolution fusion | flops 2273067008 | bytes 5386280 | tf_op jit(solution)/shard_map/conv_general_dilated | solution.py:44
  60.5 0.7 multiply_convert_fusion.2
  61.2 1.3 collective-permute-start.5
  62.5 6.2 %collective-permute-start.4 = (bf16[1,16,16,256]{3,1,2,0:T(8,128)(2,1)}, bf16[1,16,16,256]{3,1,2,0:T(8,128)(2,1)}, u32[]{:S(2)}, u32[]{:S(2)}) collective-permute-start(bf16[1,16,16,256]{3,1,2,0:T(8,128)(2,1)} %multiply_convert_fusion.2), channel_id=1, source_target_pairs={{0,2},{2,4},{4,6},{6,8},{8,10},{10,12},{12,14},{1,3},{3,5},{5,7},{... | collective-permute-start | bytes 393224 | tf_op jit(solution)/shard_map/ppermute | solution.py:12
  69.2 0.7 fusion.114
  69.9 0.5 copy.171
  70.4 0.4 fusion.87
  70.8 0.9 fusion.150
  71.7 1.3 collective-permute-start.13
  73.0 5.7 %collective-permute-start.12 = (bf16[1,32,32,128]{3,1,2,0:T(8,128)(2,1)}, bf16[1,32,32,128]{3,1,2,0:T(8,128)(2,1)}, u32[]{:S(2)}, u32[]{:S(2)}) collective-permute-start(bf16[1,32,32,128]{3,1,2,0:T(8,128)(2,1)} %get-tuple-element.33), channel_id=1, source_target_pairs={{0,2},{2,4},{4,6},{6,8},{8,10},{10,12},{12,14},{1,3},{3,5},{5,7},{... | collective-permute-start | bytes 786440 | tf_op jit(solution)/shard_map/ppermute | solution.py:12
  78.9 2.0 fusion.50
  81.0 1.8 copy.187
  82.8 2.9 %reshape.213 = f32[1024,256]{1,0:T(8,128)} reshape(f32[128,2,2,2,256]{4,3,2,1,0:T(2,128)} %copy.187) | data formatting | bytes 2097152 | tf_op jit(solution)/shard_map/reshape | solution.py:141
  85.7 0.4 fusion.80
  86.1 18.5 %fusion.10 = f32[128,3,3,3,128]{4,0,3,2,1:T(8,128)} fusion(bf16[1,4,34,34,128]{4,3,2,1,0:T(8,128)(2,1)} %get-tuple-element.27, bf16[2,32,32,128,1]{3,1,2,0,4:T(8,128)(2,1)S(1)} %fusion.80), kind=kOutput, calls=%fused_computation.15 | convolution fusion | flops 1811939328 | bytes 3477504 | tf_op jit(solution)/shard_map/conv_general_dilated | solution.py:44
  104.8 0.7 squeeze.29
  105.5 1.0 copy.190
  106.6 1.1 pad_maximum_fusion.5
  107.6 1.3 collective-permute-start.7
  108.9 3.0 %collective-permute-start.6 = (bf16[3,1,16,256]{3,1,2,0:T(2,128)(2,1)S(1)}, bf16[3,1,16,256]{3,1,2,0:T(2,128)(2,1)S(1)}, u32[]{:S(2)}, u32[]{:S(2)}) collective-permute-start(bf16[3,1,16,256]{3,1,2,0:T(2,128)(2,1)S(1)} %get-tuple-element.39), channel_id=1, source_target_pairs={{0,1},{2,3},{4,5},{6,7},{8,9},{10,11},{12,13},{14,15},{16,17},{18,... | collective-permute-start | bytes 73736 | tf_op jit(solution)/shard_map/ppermute | solution.py:12
  112.0 0.7 multiply_convert_fusion.1
  112.7 2.7 %copy.181 = f32[128,3,3,3,128]{4,3,2,1,0:T(4,128)S(1)} copy(f32[128,3,3,3,128]{4,0,3,2,1:T(8,128)} %fusion.10) | data formatting | bytes 3538944 | tf_op jit(solution)/shard_map/conv_general_dilated | solution.py:44
  115.4 2.3 %reshape.212 = f32[3456,128]{1,0:T(8,128)} reshape(f32[128,3,3,3,128]{4,3,2,1,0:T(4,128)S(1)} %copy.181) | data formatting | bytes 3538944 | tf_op jit(solution)/shard_map/reshape | solution.py:100
  117.7 6.7 %all-to-all-start = ((bf16[256,16,16]{0,2,1:T(8,128)(2,1)}), bf16[256,16,16]{0,2,1:T(8,128)(2,1)S(1)}, u32[]{:S(2)}, u32[]{:S(2)}) async-start(bf16[256,16,16]{0,2,1:T(8,128)(2,1)} %multiply_convert_fusion.1), calls=%async_computation.1 | async-start | bytes 262144 | tf_op jit(solution)/shard_map/all_to_all | solution.py:168
  124.4 0.4 reduce-scatter.7.cloned.1.call-start
  125.1 1.4 fusion.97
  126.9 0.4 copy-done.12
  127.3 3.9 %fusion.59 = bf16[1,16,8,3,256]{4,2,3,1,0:T(8,128)(2,1)S(1)} fusion(bf16[256,3,3,3,256]{4,3,2,1,0:T(4,128)(2,1)} %reshape.211, bf16[3,18,1,7,2,256]{5,3,4,1,0,2:T(8,128)(2,1)S(1)} %slice.66, bf16[3,18,1,8,3,256]{5,3,4,1,0,2:T(8,128)(2,1)S(1)} %copy.162, pred[8,3]{0,1:T(4,128)(4,1)S(1)} %copy-done.12), kind=kOutput, calls=%fused_computation.62 | convolution fusion | flops 1362468864 | bytes 4786200 | tf_op jit(solution)/shard_map/conv_general_dilated | solution.py:44
  131.3 0.7 copy.196
  132.0 0.4 all-to-all-done
  132.4 0.7 reshape_transpose_reshape.3
  133.1 1.1 pad_maximum_fusion.2
  134.2 1.3 collective-permute-start.15
  135.5 3.0 %collective-permute-start.14 = (bf16[4,1,32,128]{3,1,2,0:T(2,128)(2,1)S(1)}, bf16[4,1,32,128]{3,1,2,0:T(2,128)(2,1)S(1)}, u32[]{:S(2)}, u32[]{:S(2)}) collective-permute-start(bf16[4,1,32,128]{3,1,2,0:T(2,128)(2,1)S(1)} %get-tuple-element.29), channel_id=1, source_target_pairs={{0,1},{2,3},{4,5},{6,7},{8,9},{10,11},{12,13},{14,15},{16,17},{18,... | collective-permute-start | bytes 98312 | tf_op jit(solution)/shard_map/ppermute | solution.py:12
  138.5 0.6 pad_bitcast_fusion
  139.2 6.8 %copy.193 = bf16[1,10,34,18,16]{4,0,3,2,1:T(2,128)(2,1)} copy(bf16[1,10,34,18,16]{3,2,1,4,0:T(8,128)(2,1)S(1)} %pad_bitcast_fusion) | data formatting | bytes 391680 | tf_op jit(solution)/shard_map/broadcast_in_dim | solution.py:92
  146.0 1.7 fusion.33
  148.4 0.9 copy-done.5
  149.3 4.8 %fusion.45 = bf16[2,32,8,5,128]{4,2,3,1,0:T(8,128)(2,1)S(1)} fusion(bf16[4,34,1,7,2,128]{5,3,4,1,0,2:T(8,128)(2,1)S(1)} %slice.75, bf16[4,34,1,8,5,128]{5,3,4,1,0,2:T(8,128)(2,1)S(1)} %copy.175, pred[8,5]{0,1:T(8,128)(4,1)S(1)} %copy-done.14, bf16[128,3,3,3,128]{4,3,2,1,0:T(4,128)(2,1)S(1)} %copy-done.5), kind=kOutput, calls=%fused_computation.52 | convolution fusion | flops 2271428608 | bytes 3420200 | tf_op jit(solution)/shard_map/conv_general_dilated | solution.py:44
  154.2 1.0 copy.197
  155.2 1.0 copy-done.2
  156.2 27.9 %fusion = f32[16,3,3,3,256]{4,0,3,2,1:T(8,128)S(1)} fusion(bf16[1,10,34,18,16]{4,0,3,2,1:T(2,128)(2,1)S(1)} %copy-done.2, bf16[8,32,16,256,1]{3,2,1,0,4:T(8,128)(2,1)} %bitcast.149), kind=kOutput, calls=%fused_computation | convolution fusion | flops 905969664 | bytes 2735360 | tf_op jit(solution)/shard_map/conv_general_dilated | solution.py:44
  184.4 1.0 reshape.215
  185.4 25.1 %reduce-scatter.7.cloned.1.call-done = f32[216,128]{1,0:T(8,128)} async-done(((f32[3456,128]{1,0:T(8,128)}), f32[216,128]{1,0:T(8,128)}) %reduce-scatter.7.cloned.1.call-update) | async-done | bytes 110608
  (86 shorter events, 5.5 us)
Async XLA Ops:
  7.2 12.7 %copy-start.10 = (bf16[1,16,16,256]{3,2,1,0:T(8,128)(2,1)S(1)}, bf16[1,16,16,256]{3,2,1,0:T(8,128)(2,1)}, u32[]{:S(2)}) copy-start(bf16[1,16,16,256]{3,2,1,0:T(8,128)(2,1)} %param.9) | copy-start | bytes 393220
  7.2 148.0 %all-gather.2.cloned.1.call-start = ((), (), s32[]{:S(2)}) async-start(), calls=%async_computation.4 | async-start | bytes 2228224 | tf_op jit(solution)/shard_map/all_gather | solution.py:158
  7.2 12.6 %collective-permute-start.8 = (bf16[1,16,16,256]{3,2,1,0:T(8,128)(2,1)}, bf16[1,16,16,256]{3,2,1,0:T(8,128)(2,1)S(1)}, u32[]{:S(2)}, u32[]{:S(2)}) collective-permute-start(bf16[1,16,16,256]{3,2,1,0:T(8,128)(2,1)} %param.9), channel_id=1, source_target_pairs={{0,2},{2,4},{4,6},{6,8},{8,10},{10,12},{12,14},{1,3},{3,5},{5,7},{... | collective-permute-start | bytes 393224 | tf_op jit(solution)/shard_map/ppermute | solution.py:12
  12.1 7.8 %collective-permute-start.9 = (bf16[1,16,16,256]{3,2,1,0:T(8,128)(2,1)}, bf16[1,16,16,256]{3,2,1,0:T(8,128)(2,1)S(1)}, u32[]{:S(2)}, u32[]{:S(2)}) collective-permute-start(bf16[1,16,16,256]{3,2,1,0:T(8,128)(2,1)} %param.9), channel_id=1, source_target_pairs={{2,0},{4,2},{6,4},{8,6},{10,8},{12,10},{14,12},{3,1},{5,3},{7,5},{... | collective-permute-start | bytes 393224 | tf_op jit(solution)/shard_map/ppermute | solution.py:15
  15.3 24.5 %collective-permute-start = (bf16[1,32,32,128]{3,2,1,0:T(8,128)(2,1)}, bf16[1,32,32,128]{3,2,1,0:T(8,128)(2,1)S(1)}, u32[]{:S(2)}, u32[]{:S(2)}) collective-permute-start(bf16[1,32,32,128]{3,2,1,0:T(8,128)(2,1)} %get-tuple-element.36), channel_id=1, source_target_pairs={{0,2},{2,4},{4,6},{6,8},{8,10},{10,12},{12,14},{1,3},{3,5},{5,7},{... | collective-permute-start | bytes 786440 | tf_op jit(solution)/shard_map/ppermute | solution.py:12
  20.5 17.4 %collective-permute-start.11 = (bf16[3,1,16,256]{3,2,1,0:T(8,128)(2,1)}, bf16[3,1,16,256]{3,2,1,0:T(8,128)(2,1)}, u32[]{:S(2)}, u32[]{:S(2)}) collective-permute-start(bf16[3,1,16,256]{3,2,1,0:T(8,128)(2,1)} %get-tuple-element.38), channel_id=1, source_target_pairs={{1,0},{3,2},{5,4},{7,6},{9,8},{11,10},{13,12},{15,14},{17,16},{19,... | collective-permute-start | bytes 73736 | tf_op jit(solution)/shard_map/ppermute | solution.py:15
  21.8 16.1 %collective-permute-start.10 = (bf16[3,1,16,256]{3,2,1,0:T(8,128)(2,1)S(1)}, bf16[3,1,16,256]{3,2,1,0:T(8,128)(2,1)}, u32[]{:S(2)}, u32[]{:S(2)}) collective-permute-start(bf16[3,1,16,256]{3,2,1,0:T(8,128)(2,1)S(1)} %get-tuple-element.37), channel_id=1, source_target_pairs={{0,1},{2,3},{4,5},{6,7},{8,9},{10,11},{12,13},{14,15},{16,17},{18,... | collective-permute-start | bytes 73736 | tf_op jit(solution)/shard_map/ppermute | solution.py:12
  26.0 14.6 %collective-permute-start.1 = (bf16[1,32,32,128]{3,2,1,0:T(8,128)(2,1)}, bf16[1,32,32,128]{3,2,1,0:T(8,128)(2,1)}, u32[]{:S(2)}, u32[]{:S(2)}) collective-permute-start(bf16[1,32,32,128]{3,2,1,0:T(8,128)(2,1)} %get-tuple-element.35), channel_id=1, source_target_pairs={{2,0},{4,2},{6,4},{8,6},{10,8},{12,10},{14,12},{3,1},{5,3},{7,5},{... | collective-permute-start | bytes 786440 | tf_op jit(solution)/shard_map/ppermute | solution.py:15
  27.3 9.0 %copy-start.9 = (bf16[1024,256]{1,0:T(8,128)(2,1)S(1)}, bf16[1024,256]{1,0:T(8,128)(2,1)}, u32[]{:S(2)}) copy-start(bf16[1024,256]{1,0:T(8,128)(2,1)} %param.7) | copy-start | bytes 1572868
  27.3 158.0 %reduce-scatter.5.cloned.1.call-start = ((), (), s32[]{:S(2)}) async-start(), calls=%async_computation.3 | async-start | bytes 1114112 | tf_op jit(solution)/shard_map/reduce_scatter | solution.py:188
  36.3 1.2 copy-start.8
  37.9 15.9 %copy-start.4 = (bf16[128,3,3,3,128]{4,3,2,1,0:T(4,128)(2,1)}, bf16[128,3,3,3,128]{4,3,2,1,0:T(4,128)(2,1)S(1)}, u32[]{:S(2)}) copy-start(bf16[128,3,3,3,128]{4,3,2,1,0:T(4,128)(2,1)S(1)} %reshape.209) | copy-start | bytes 2654212
  39.5 1.0 copy-start.3
  39.7 6.8 %copy-start.11 = (pred[8,3]{0,1:T(4,128)(4,1)S(1)}, pred[8,3]{0,1:T(4,128)(4,1)}, u32[]{:S(2)}) copy-start(pred[8,3]{0,1:T(4,128)(4,1)} %constant.41) | copy-start | bytes 76
  41.6 9.0 %collective-permute-start.3 = (bf16[4,1,32,128]{3,2,1,0:T(8,128)(2,1)S(1)}, bf16[4,1,32,128]{3,2,1,0:T(8,128)(2,1)S(1)}, u32[]{:S(2)}, u32[]{:S(2)}) collective-permute-start(bf16[4,1,32,128]{3,2,1,0:T(8,128)(2,1)S(1)} %get-tuple-element.32), channel_id=1, source_target_pairs={{1,0},{3,2},{5,4},{7,6},{9,8},{11,10},{13,12},{15,14},{17,16},{19,... | collective-permute-start | bytes 98312 | tf_op jit(solution)/shard_map/ppermute | solution.py:15
  42.9 7.7 %collective-permute-start.2 = (bf16[4,1,32,128]{3,2,1,0:T(8,128)(2,1)S(1)}, bf16[4,1,32,128]{3,2,1,0:T(8,128)(2,1)S(1)}, u32[]{:S(2)}, u32[]{:S(2)}) collective-permute-start(bf16[4,1,32,128]{3,2,1,0:T(8,128)(2,1)S(1)} %get-tuple-element.31), channel_id=1, source_target_pairs={{0,1},{2,3},{4,5},{6,7},{8,9},{10,11},{12,13},{14,15},{16,17},{18,... | collective-permute-start | bytes 98312 | tf_op jit(solution)/shard_map/ppermute | solution.py:12
  53.4 0.7 copy-start.13
  60.3 8.4 %copy-start.6 = (f32[1,16,8,2,256]{4,2,3,1,0:T(8,128)}, f32[1,16,8,2,256]{4,2,3,1,0:T(8,128)S(1)}, u32[]{:S(2)}) copy-start(f32[1,16,8,2,256]{4,2,3,1,0:T(8,128)S(1)} %get-tuple-element.43) | copy-start | bytes 786436
  61.2 45.4 %collective-permute-start.5 = (bf16[1,16,16,256]{3,1,2,0:T(8,128)(2,1)}, bf16[1,16,16,256]{3,1,2,0:T(8,128)(2,1)}, u32[]{:S(2)}, u32[]{:S(2)}) collective-permute-start(bf16[1,16,16,256]{3,1,2,0:T(8,128)(2,1)} %multiply_convert_fusion.2), channel_id=1, source_target_pairs={{2,0},{4,2},{6,4},{8,6},{10,8},{12,10},{14,12},{3,1},{5,3},{7,5},{... | collective-permute-start | bytes 393224 | tf_op jit(solution)/shard_map/ppermute | solution.py:15
  62.5 44.1 %collective-permute-start.4 = (bf16[1,16,16,256]{3,1,2,0:T(8,128)(2,1)}, bf16[1,16,16,256]{3,1,2,0:T(8,128)(2,1)}, u32[]{:S(2)}, u32[]{:S(2)}) collective-permute-start(bf16[1,16,16,256]{3,1,2,0:T(8,128)(2,1)} %multiply_convert_fusion.2), channel_id=1, source_target_pairs={{0,2},{2,4},{4,6},{6,8},{8,10},{10,12},{12,14},{1,3},{3,5},{5,7},{... | collective-permute-start | bytes 393224 | tf_op jit(solution)/shard_map/ppermute | solution.py:12
  70.8 8.1 %copy-start = (bf16[2,32,32,128]{3,1,2,0:T(8,128)(2,1)}, bf16[2,32,32,128]{3,1,2,0:T(8,128)(2,1)S(1)}, u32[]{:S(2)}) copy-start(bf16[2,32,32,128]{3,1,2,0:T(8,128)(2,1)S(1)} %fusion.87) | copy-start | bytes 1572868
  71.7 61.4 %collective-permute-start.13 = (bf16[1,32,32,128]{3,1,2,0:T(8,128)(2,1)}, bf16[1,32,32,128]{3,1,2,0:T(8,128)(2,1)}, u32[]{:S(2)}, u32[]{:S(2)}) collective-permute-start(bf16[1,32,32,128]{3,1,2,0:T(8,128)(2,1)} %get-tuple-element.34), channel_id=1, source_target_pairs={{2,0},{4,2},{6,4},{8,6},{10,8},{12,10},{14,12},{3,1},{5,3},{7,5},{... | collective-permute-start | bytes 786440 | tf_op jit(solution)/shard_map/ppermute | solution.py:15
  73.0 60.1 %collective-permute-start.12 = (bf16[1,32,32,128]{3,1,2,0:T(8,128)(2,1)}, bf16[1,32,32,128]{3,1,2,0:T(8,128)(2,1)}, u32[]{:S(2)}, u32[]{:S(2)}) collective-permute-start(bf16[1,32,32,128]{3,1,2,0:T(8,128)(2,1)} %get-tuple-element.33), channel_id=1, source_target_pairs={{0,2},{2,4},{4,6},{6,8},{8,10},{10,12},{12,14},{1,3},{3,5},{5,7},{... | collective-permute-start | bytes 786440 | tf_op jit(solution)/shard_map/ppermute | solution.py:12
  86.1 18.5 %copy-start.7 = (f32[1,16,8,2,256]{4,2,3,1,0:T(8,128)S(1)}, f32[1,16,8,2,256]{4,2,3,1,0:T(8,128)}, u32[]{:S(2)}) copy-start(f32[1,16,8,2,256]{4,2,3,1,0:T(8,128)} %copy-done.6) | copy-start | bytes 786436
  107.6 17.5 %collective-permute-start.7 = (bf16[3,1,16,256]{3,1,2,0:T(2,128)(2,1)S(1)}, bf16[3,1,16,256]{3,1,2,0:T(2,128)(2,1)S(1)}, u32[]{:S(2)}, u32[]{:S(2)}) collective-permute-start(bf16[3,1,16,256]{3,1,2,0:T(2,128)(2,1)S(1)} %get-tuple-element.40), channel_id=1, source_target_pairs={{1,0},{3,2},{5,4},{7,6},{9,8},{11,10},{13,12},{15,14},{17,16},{19,... | collective-permute-start | bytes 73736 | tf_op jit(solution)/shard_map/ppermute | solution.py:15
  108.9 16.2 %collective-permute-start.6 = (bf16[3,1,16,256]{3,1,2,0:T(2,128)(2,1)S(1)}, bf16[3,1,16,256]{3,1,2,0:T(2,128)(2,1)S(1)}, u32[]{:S(2)}, u32[]{:S(2)}) collective-permute-start(bf16[3,1,16,256]{3,1,2,0:T(2,128)(2,1)S(1)} %get-tuple-element.39), channel_id=1, source_target_pairs={{0,1},{2,3},{4,5},{6,7},{8,9},{10,11},{12,13},{14,15},{16,17},{18,... | collective-permute-start | bytes 73736 | tf_op jit(solution)/shard_map/ppermute | solution.py:12
  117.7 14.6 %all-to-all-start = ((bf16[256,16,16]{0,2,1:T(8,128)(2,1)}), bf16[256,16,16]{0,2,1:T(8,128)(2,1)S(1)}, u32[]{:S(2)}, u32[]{:S(2)}) async-start(bf16[256,16,16]{0,2,1:T(8,128)(2,1)} %multiply_convert_fusion.1), calls=%async_computation.1 | async-start | bytes 262144 | tf_op jit(solution)/shard_map/all_to_all | solution.py:168
  124.4 86.1 %reduce-scatter.7.cloned.1.call-start = ((), (), s32[]{:S(2)}) async-start(), calls=%async_computation.5 | async-start | bytes 1880064
  126.6 0.7 copy-start.12
  131.2 1.9 copy-start.1
  134.2 11.8 %collective-permute-start.15 = (bf16[4,1,32,128]{3,1,2,0:T(2,128)(2,1)S(1)}, bf16[4,1,32,128]{3,1,2,0:T(2,128)(2,1)S(1)}, u32[]{:S(2)}, u32[]{:S(2)}) collective-permute-start(bf16[4,1,32,128]{3,1,2,0:T(2,128)(2,1)S(1)} %get-tuple-element.30), channel_id=1, source_target_pairs={{1,0},{3,2},{5,4},{7,6},{9,8},{11,10},{13,12},{15,14},{17,16},{19,... | collective-permute-start | bytes 98312 | tf_op jit(solution)/shard_map/ppermute | solution.py:15
  135.5 10.5 %collective-permute-start.14 = (bf16[4,1,32,128]{3,1,2,0:T(2,128)(2,1)S(1)}, bf16[4,1,32,128]{3,1,2,0:T(2,128)(2,1)S(1)}, u32[]{:S(2)}, u32[]{:S(2)}) collective-permute-start(bf16[4,1,32,128]{3,1,2,0:T(2,128)(2,1)S(1)} %get-tuple-element.29), channel_id=1, source_target_pairs={{0,1},{2,3},{4,5},{6,7},{8,9},{10,11},{12,13},{14,15},{16,17},{18,... | collective-permute-start | bytes 98312 | tf_op jit(solution)/shard_map/ppermute | solution.py:12
  148.0 1.3 copy-start.5
  148.0 1.3 copy-start.14
  154.1 2.1 copy-start.2
Sparse Core Ops, SparseCore 0:
  27.4 44.9 all-gather.1
  86.3 60.1 reduce-scatter.4
  151.3 59.1 reduce-scatter.6
where the time goes:
time: 221 us; the launch traced here: 217 us
  matrix products  67.4 us (30%)
  starting transfers between devices  52.7 us (24%)
  local copies, waits for them, and re-layouts  46 us (21%)
  waiting for transfers between devices  25.9 us (12%)
  between operations  14.7 us (7%)
  other arithmetic  10.6 us (5%)
    conv_general_dilated x9, matrix products, correlate(): lax.conv_general_dilated(left, right, strides, padding, lhs_dilation=left...  67.4 us
    ppermute x8, starting transfers between devices, extended(): lax.ppermute(lax.slice_in_dim(block, block.shape[dim] - width, None, axis...  35.2 us
    unnamed x4, waiting for transfers between devices  25.4 us
    ppermute x8, starting transfers between devices, extended(): lax.ppermute(lax.slice_in_dim(block, 0, width, axis=dim), axis, backward)  10.3 us
    reshape x2, local copies, waits for them, and re-layouts, convolve(): kernel = weight_collection.reshape(in_width, 3, 3, 3, out_width)  9.34 us
    broadcast_in_dim x2, local copies, waits for them, and re-layouts, kernel_grad(): padded[None]  7.49 us
    conv_general_dilated x17, local copies, waits for them, and re-layouts, correlate(): lax.conv_general_dilated(left, right, strides, padding, lhs_dilation=left...  7.43 us
    all_to_all x1, starting transfers between devices, body(): lax.all_to_all(hidden_lower.reshape(lower_voxels, lower_width), ('sx', 's...  6.7 us
  transfers between devices with their start and end apart: 20, of which 2 were waited for; matrix products, arithmetic and copies ran while one was open for 55% of the time, Pallas kernels for 0%

commit v1 on v0

--- a/solution.py
+++ b/solution.py
@@ -1,6 +1,10 @@
+import functools
+
 import jax
 import jax.numpy as jnp
 from jax import lax
+from jax.experimental import pallas as pl
+from jax.experimental.pallas import tpu as pltpu
 from jax.sharding import PartitionSpec as P
 
 
@@ -191,6 +195,410 @@
     return (bottleneck, grad_feature, upper_rows, down_rows, lower_rows)
 
 
+BF, F32 = jnp.bfloat16, jnp.float32
+MESH_ID = pl.DeviceIdType.MESH
+NT = (((1,), (1,)), ((), ()))
+TN = (((0,), (0,)), ((), ()))
+
+
+def mm(left, right, dims=(((1,), (0,)), ((), ()))):
+    return lax.dot_general(left, right, dims, preferred_element_type=F32)
+
+
+def depth_taps(block, depth):
+    wide = block.astype(F32)
+    rows = wide.shape[0]
+    at = lax.broadcasted_iota(jnp.int32, wide.shape, 0) % depth
+    before = jnp.where(at == 0, 0.0, pltpu.roll(wide, 1, 0)).astype(BF)
+    after = jnp.where(at == depth - 1, 0.0, pltpu.roll(wide, rows - 1, 0)).astype(BF)
+    return before, block, after
+
+
+def fused(n_sx, feat, wu, dw, wl, cot, bott, gfeat, gup, gdown, glow,
+          fx, gx, hx, cx, call, ht, htr, xz, gz, hz, cz, wf, wb, wlf, wlb, wd, wtl, su, sd,
+          pu, hu, gzt, hcat, ghl, pl_low, hp, at, gl, s1, r1, s2, r2,
+          f_s, f_r, g_s, g_r, h_s, h_r, c_s, c_r, ca_s, ca_r, cf_s, cf_r, t_s, t_r,
+          a_s, a_r, b_s, b_r):
+    g, i, j = lax.axis_index("groups"), lax.axis_index("sx"), lax.axis_index("sy")
+    k = 1 - j
+    me = 2 * i + j
+    total = 2 * n_sx
+
+    def remote(src, dst, ss, rs, dev):
+        return pltpu.make_async_remote_copy(
+            src_ref=src, dst_ref=dst, send_sem=ss, recv_sem=rs, device_id=dev,
+            device_id_type=MESH_ID)
+
+    def guard(cond, f):
+        if cond is None:
+            f()
+        else:
+            pl.when(cond)(f)
+
+    low, high = i > 0, i < n_sx - 1
+    down_dev = lambda s: (g, jnp.maximum(i - 1, 0), s)
+    up_dev = lambda s: (g, jnp.minimum(i + 1, n_sx - 1), s)
+
+    def halo(buf, nx, ny, ss, rs):
+        ysrc = ny - j * (ny - 1)
+        ydst = j * (ny + 1)
+        yrcv = k * (ny + 1)
+        body = pl.ds(1, ny)
+        slabs = pl.ds(1, nx)
+        sends = [
+            (low, buf.at[1, body], buf.at[nx + 1, body], down_dev(j)),
+            (high, buf.at[nx, body], buf.at[0, body], up_dev(j)),
+            (None, buf.at[slabs, ysrc], buf.at[slabs, ydst], (g, i, k)),
+            (low, buf.at[1, ysrc], buf.at[nx + 1, ydst], down_dev(k)),
+            (high, buf.at[nx, ysrc], buf.at[0, ydst], up_dev(k)),
+        ]
+        recvs = [
+            (high, buf.at[nx + 1, body]),
+            (low, buf.at[0, body]),
+            (None, buf.at[slabs, yrcv]),
+            (high, buf.at[nx + 1, yrcv]),
+            (low, buf.at[0, yrcv]),
+        ]
+
+        def start():
+            for m, (cond, src, dst, dev) in enumerate(sends):
+                guard(cond, lambda m=m, src=src, dst=dst, dev=dev: remote(
+                    src, dst, ss.at[m], rs.at[m], dev).start())
+
+        def wait():
+            for m, (cond, dst) in enumerate(recvs):
+                guard(cond, lambda m=m, dst=dst: remote(
+                    dst, dst, ss.at[m], rs.at[m], (g, i, k)).wait_recv())
+
+        def done():
+            for m, (cond, src, dst, dev) in enumerate(sends):
+                guard(cond, lambda m=m, src=src, dst=dst, dev=dev: remote(
+                    src, dst, ss.at[m], rs.at[m], dev).wait_send())
+
+        return start, wait, done
+
+    def edges(buf, nx, ny):
+        zero_row = jnp.zeros(buf.shape[2:], BF)
+        for s in range(nx + 2):
+            buf[s, j * (ny + 1)] = zero_row
+
+        @pl.when(i == 0)
+        def _():
+            buf[0] = jnp.zeros(buf.shape[1:], BF)
+
+        @pl.when(i == n_sx - 1)
+        def _():
+            buf[nx + 1] = jnp.zeros(buf.shape[1:], BF)
+
+    barrier = pltpu.get_barrier_semaphore()
+    for q in range(1, total):
+        other = lax.rem(me + q, total)
+        pl.semaphore_signal(barrier, inc=1, device_id=(g, other // 2, other % 2),
+                            device_id_type=MESH_ID)
+    for s in range(2):
+        fx[1 + s, 1:33] = feat[s]
+    cx[1, 1:17] = cot[...].reshape(16, 16, 256)
+    call[me] = cot[...]
+    pl.semaphore_wait(barrier, total - 1)
+
+    f_start, f_wait, f_done = halo(fx, 2, 32, f_s, f_r)
+    g_start, g_wait, g_done = halo(gx, 2, 32, g_s, g_r)
+    h_start, h_wait, h_done = halo(hx, 1, 16, h_s, h_r)
+    c_start, c_wait, c_done = halo(cx, 1, 16, c_s, c_r)
+    c_start()
+    f_start()
+    edges(fx, 2, 32)
+    edges(gx, 2, 32)
+    edges(hx, 1, 16)
+    edges(cx, 1, 16)
+
+    def widen_lower(s, _):
+        rows = pl.ds(s * 256, 256)
+        for h in range(2):
+            wtl[h, rows] = wl[rows, h * 128:(h + 1) * 128].astype(F32)
+        return 0
+    lax.fori_loop(0, 27, widen_lower, 0)
+    for t in range(27):
+        for h in range(2):
+            tap = wtl[h, pl.ds(t, 256, stride=27), :].astype(BF)
+            e = t % 3
+            wlf[t // 3, e * 256:(e + 1) * 256, h * 128:(h + 1) * 128] = tap
+            u = 26 - t
+            f = u % 3
+            wlb[u // 3, :, f * 256 + h * 128:f * 256 + (h + 1) * 128] = tap
+
+    c_wait()
+
+    def lower_taps(src, dst):
+        for s in range(3):
+            parts = depth_taps(src[s].reshape(18 * 16, 256), 16)
+            for e in range(3):
+                dst[s, :, :, e * 256:(e + 1) * 256] = parts[e].reshape(18, 16, 256)
+    lower_taps(cx, cz)
+    acc = jnp.zeros((256, 256), F32)
+    for ab in range(9):
+        acc += mm(cz[ab // 3, ab % 3:ab % 3 + 16].reshape(256, 768), wlb[ab], NT)
+    ghl[...] = acc
+
+    su[...] = wu[...].astype(F32)
+    for t in range(27):
+        tap = su[pl.ds(t, 128, stride=27), :].astype(BF)
+        e, u = t % 3, 26 - t
+        f = u % 3
+        wf[t // 3, e * 128:(e + 1) * 128, :] = tap
+        wb[u // 3, :, f * 128:(f + 1) * 128] = tap
+    for h in range(2):
+        sd[h] = dw[:, h * 128:(h + 1) * 128].astype(F32)
+    for c in range(8):
+        for h in range(2):
+            wd[c * 128:(c + 1) * 128, h * 128:(h + 1) * 128] = (
+                sd[h, pl.ds(c, 128, stride=8), :].astype(BF))
+
+    f_wait()
+
+    def gather_copy(q):
+        to = lax.rem(i + q, n_sx)
+        return remote(call.at[me], call.at[me], ca_s.at[q], ca_r.at[q], (g, to, j))
+
+    def gather_recv(q):
+        frm = lax.rem(i - q + n_sx, n_sx)
+        blk = call.at[2 * frm + j]
+        return remote(blk, blk, ca_s.at[q], ca_r.at[q], (g, i, k))
+
+    def forward_copy(q):
+        frm = lax.rem(i - q + n_sx, n_sx)
+        blk = call.at[2 * frm + j]
+        return remote(blk, blk, cf_s.at[q], cf_r.at[q], (g, i, k))
+
+    def forward_recv(q):
+        frm = lax.rem(i - q + n_sx, n_sx)
+        blk = call.at[2 * frm + k]
+        return remote(blk, blk, cf_s.at[q], cf_r.at[q], (g, i, k))
+
+    for q in range(1, n_sx):
+        gather_copy(q).start()
+    forward_copy(0).start()
+
+    def upper_taps(src, dst, s, y0, ny):
+        parts = depth_taps(src[s, pl.ds(y0, ny)].reshape(ny * 32, 128), 32)
+        for e in range(3):
+            dst[s, pl.ds(y0, ny), :, e * 128:(e + 1) * 128] = parts[e].reshape(ny, 32, 128)
+
+    def upper_slab(s, _):
+        upper_taps(fx, xz, s, 0, 34)
+        return 0
+    lax.fori_loop(0, 4, upper_slab, 0)
+
+    def conv_up(m, _):
+        s, y0 = m // 2, (m % 2) * 16
+        acc = jnp.zeros((512, 128), F32)
+        for ab in range(9):
+            lhs = xz[s + ab // 3, pl.ds(y0 + ab % 3, 16)].reshape(512, 384)
+            acc += mm(lhs, wf[ab])
+        pu[s, pl.ds(y0, 16)] = acc.reshape(16, 32, 128)
+        hid = (acc * jax.nn.sigmoid(acc)).astype(BF).astype(F32)
+        hu[s, pl.ds(y0 // 2, 8)] = hid.reshape(8, 2, 32, 128)
+        return 0
+    lax.fori_loop(0, 4, conv_up, 0)
+
+    for c in range(8):
+        ii, jj, ll = c // 4, c // 2 % 2, c % 2
+        hcat[:, c * 128:(c + 1) * 128] = (
+            hu[ii, :, jj, pl.ds(ll, 16, stride=2), :].reshape(256, 128).astype(BF))
+    pre = mm(hcat[...], wd[...])
+    sig = jax.nn.sigmoid(pre)
+    hid_low = pre * sig
+    ht[...] = hid_low.T.astype(BF)
+    hx[1, 1:17] = hid_low.astype(BF).reshape(16, 16, 256)
+    gpl = (ghl[...] * (sig * (1.0 + pre * (1.0 - sig)))).astype(BF)
+    pl_low[...] = gpl
+    h_start()
+
+    def turn_copy(q):
+        other = lax.rem(me + q, total)
+        return remote(ht.at[pl.ds(16 * other, 16)], htr.at[me], t_s.at[q], t_r.at[q],
+                      (g, other // 2, other % 2))
+
+    def turn_recv(q):
+        frm = lax.rem(me - q + total, total)
+        return remote(htr.at[frm], htr.at[frm], t_s.at[q], t_r.at[q], (g, i, k))
+    for q in range(1, total):
+        turn_copy(q).start()
+    htr[me] = ht[pl.ds(pl.multiple_of(16 * me, 16), 16)]
+
+    for c in range(8):
+        ii, jj, ll = c // 4, c // 2 % 2, c % 2
+        back = mm(gpl, wd[c * 128:(c + 1) * 128, :], NT)
+        hu[ii, :, jj, pl.ds(ll, 16, stride=2), :] = back.reshape(16, 16, 128)
+
+    def grad_pre(m, _):
+        s, y0 = m // 4, (m % 4) * 8
+        v = pu[s, pl.ds(y0, 8)]
+        sg = jax.nn.sigmoid(v)
+        grad = hu[s, pl.ds(y0 // 2, 4)].reshape(8, 32, 128) * (sg * (1.0 + v * (1.0 - sg)))
+        gx[s + 1, pl.ds(y0 + 1, 8)] = grad.astype(BF)
+        return 0
+    lax.fori_loop(0, 8, grad_pre, 0)
+    g_start()
+
+    for s in range(2):
+        upper_taps(gx, gz, s + 1, 1, 32)
+        for e in range(3):
+            col = gz[s + 1, 1:33, :, e * 128:(e + 1) * 128].reshape(1024, 128)
+            gzt[e * 128:(e + 1) * 128, s * 1024:(s + 1) * 1024] = col.T
+
+    dgrad = mm(hcat[...], pl_low[...], TN)
+    for c in range(8):
+        for h in range(2):
+            sd[h, pl.ds(c, 128, stride=8), :] = dgrad[c * 128:(c + 1) * 128, h * 128:(h + 1) * 128]
+    for ab in range(9):
+        acc = jnp.zeros((384, 128), F32)
+        for s in range(2):
+            rhs = fx[s + ab // 3, ab % 3:ab % 3 + 32].reshape(1024, 128)
+            acc += mm(gzt[:, s * 1024:(s + 1) * 1024], rhs)
+        for e in range(3):
+            t = ab * 3 + 2 - e
+            su[pl.ds(t, 128, stride=27), :] = acc[e * 128:(e + 1) * 128].T
+
+    for d in range(total):
+        q, s = d // 2, d % 2
+        s1[s, q, 0:216] = su[216 * d:216 * (d + 1)].astype(BF)
+        s1[s, q, 216:224] = jnp.zeros((8, 128), BF)
+        s1[s, q, 224:288] = sd[0, 64 * d:64 * (d + 1)].astype(BF)
+        s1[s, q, 288:352] = sd[1, 64 * d:64 * (d + 1)].astype(BF)
+    pair = remote(s1.at[k], r1, a_s, a_r, (g, i, k))
+    pair.start()
+
+    h_wait()
+    lower_taps(hx, hz)
+    acc = jnp.zeros((256, 256), F32)
+    for ab in range(9):
+        acc += mm(hz[ab // 3, ab % 3:ab % 3 + 16].reshape(256, 768), wlf[ab])
+    bott[...] = acc.astype(BF)
+
+    pair.wait_recv()
+    for q in range(n_sx):
+        s2[q] = (s1[j, q].astype(F32) + r1[q].astype(F32)).astype(BF)
+
+    def sum_copy(q):
+        to = lax.rem(i + q, n_sx)
+        return remote(s2.at[to], r2.at[q], b_s.at[q], b_r.at[q], (g, to, j))
+    for q in range(1, n_sx):
+        sum_copy(q).start()
+
+    for q in range(1, n_sx):
+        gather_recv(q).wait_recv()
+        forward_copy(q).start()
+
+    g_wait()
+    upper_taps(gx, gz, 0, 0, 34)
+    upper_taps(gx, gz, 3, 0, 34)
+    for s in (1, 2):
+        for y in (0, 33):
+            upper_taps(gx, gz, s, y, 1)
+
+    def conv_down(m, _):
+        s, y0 = m // 2, (m % 2) * 16
+        acc = jnp.zeros((512, 128), F32)
+        for ab in range(9):
+            lhs = gz[s + ab // 3, pl.ds(y0 + ab % 3, 16)].reshape(512, 384)
+            acc += mm(lhs, wb[ab], NT)
+        gfeat[s, pl.ds(y0, 16)] = acc.astype(BF).reshape(16, 32, 128)
+        return 0
+    lax.fori_loop(0, 4, conv_down, 0)
+
+    for q in range(1, total):
+        turn_recv(q).wait_recv()
+    hp[...] = jnp.zeros(hp.shape, F32)
+    for d in range(total):
+        hp[:, 640 + 256 * d:640 + 256 * (d + 1)] = htr[d].astype(F32)
+    lane = lax.broadcasted_iota(jnp.int32, (16, 5120), 1)
+    z, y = lane % 16, lane // 16 % 32
+    for be in range(9):
+        b, e = be // 3 - 1, be % 3 - 1
+        shift = 16 * b + e
+        moved = pltpu.roll(hp[...], (-shift) % 5376, 1)[:, 128:5248]
+        ok = (z + e >= 0) & (z + e < 16) & (y + b >= 0) & (y + b < 32)
+        moved = jnp.where(ok, moved, 0.0).astype(BF)
+        for a in range(3):
+            t = a * 9 + be
+            at[t * 16:(t + 1) * 16, :] = moved[:, 512 * a:512 * a + 4096]
+    for q in range(n_sx):
+        forward_recv(q).wait_recv()
+    acc = jnp.zeros((432, 256), F32)
+    for c in range(4):
+        acc += mm(at[:, c * 1024:(c + 1) * 1024], call[4 * c:4 * c + 4].reshape(1024, 256))
+    for t in range(27):
+        for h in range(2):
+            gl[h, pl.ds(t, 16, stride=27), :] = acc[t * 16:(t + 1) * 16, h * 128:(h + 1) * 128]
+    for h in range(2):
+        glow[:, h * 128:(h + 1) * 128] = gl[h]
+
+    rows = s2[i].astype(F32)
+    for q in range(1, n_sx):
+        blk = r2.at[q]
+        remote(blk, blk, b_s.at[q], b_r.at[q], (g, i, k)).wait_recv()
+        rows += r2[q].astype(F32)
+    gup[...] = rows[0:216]
+    gdown[:, 0:128] = rows[224:288]
+    gdown[:, 128:256] = rows[288:352]
+
+    f_done()
+    g_done()
+    h_done()
+    c_done()
+    pair.wait_send()
+    for q in range(1, n_sx):
+        gather_copy(q).wait_send()
+        sum_copy(q).wait_send()
+    for q in range(n_sx):
+        forward_copy(q).wait_send()
+    for q in range(1, total):
+        turn_copy(q).wait_send()
+
+
+def fused_body(feature, weight_upper, down_weight_matrix, weight_lower, cotangent):
+    n_sx = lax.axis_size("sx")
+    total = 2 * n_sx
+    V = pltpu.VMEM
+    S = pltpu.SemaphoreType.DMA
+    scratch = [
+        V((4, 34, 32, 128), BF), V((4, 34, 32, 128), BF), V((3, 18, 16, 256), BF),
+        V((3, 18, 16, 256), BF), V((total, 256, 256), BF), V((256, 256), BF),
+        V((total, 16, 256), BF), V((4, 34, 32, 384), BF), V((4, 34, 32, 384), BF),
+        V((3, 18, 16, 768), BF), V((3, 18, 16, 768), BF),
+        V((9, 384, 128), BF), V((9, 128, 384), BF), V((9, 768, 256), BF), V((9, 256, 768), BF),
+        V((1024, 256), BF), V((2, 6912, 128), F32), V((3456, 128), F32), V((2, 1024, 128), F32),
+        V((2, 32, 32, 128), F32), V((2, 16, 2, 32, 128), F32), V((384, 2048), BF),
+        V((256, 1024), BF), V((256, 256), F32), V((256, 256), BF),
+        V((16, 5376), F32), V((432, 4096), BF), V((2, 432, 128), F32),
+        V((2, n_sx, 352, 128), BF), V((n_sx, 352, 128), BF), V((n_sx, 352, 128), BF),
+        V((n_sx, 352, 128), BF),
+        S((5,)), S((5,)), S((5,)), S((5,)), S((5,)), S((5,)), S((5,)), S((5,)),
+        S((n_sx,)), S((n_sx,)), S((n_sx,)), S((n_sx,)), S((total,)), S((total,)),
+        S, S, S((n_sx,)), S((n_sx,)),
+    ]
+    vm = pl.BlockSpec(memory_space=pltpu.VMEM)
+    bott, gfeat, gup, gdown, glow = pl.pallas_call(
+        functools.partial(fused, n_sx),
+        out_shape=(
+            jax.ShapeDtypeStruct((256, 256), BF),
+            jax.ShapeDtypeStruct((2, 32, 32, 128), BF),
+            jax.ShapeDtypeStruct((216, 128), F32),
+            jax.ShapeDtypeStruct((64, 256), F32),
+            jax.ShapeDtypeStruct((432, 256), F32),
+        ),
+        in_specs=[vm] * 5,
+        out_specs=(vm,) * 5,
+        scratch_shapes=scratch,
+        compiler_params=pltpu.CompilerParams(
+            collective_id=0, has_side_effects=True, vmem_limit_bytes=60 * 1024 * 1024),
+        cost_estimate=pl.CostEstimate(flops=9_000_000_000, bytes_accessed=12_000_000,
+                                      transcendentals=600_000),
+    )(feature, weight_upper, down_weight_matrix, weight_lower, cotangent.reshape(256, 256))
+    return (bott.reshape(1, 16, 16, 256), gfeat, gup, gdown, glow)
+
+
 def solution(mesh):
     placed = (
         P(("groups", "sx"), "sy", None, None),
@@ -199,8 +607,9 @@
         P("groups", None),
         P(("groups", "sx"), "sy", None, None),
     )
+    fits = mesh.shape["sx"] == 8 and mesh.shape["sy"] == 2
     return jax.shard_map(
-        body,
+        fused_body if fits else body,
         mesh=mesh,
         in_specs=placed,
         out_specs=(

time: 221 us -> 92.5 us (0.42)
  the two profiles are of different devices: /device:TPU:0 before, /device:TPU:19 now
where the time goes in v1:
time: 92.5 us; the launch traced here: 92.2 us
  Pallas kernels  83.3 us (90%)
  local copies, waits for them, and re-layouts  8.26 us (9%)
    pallas_call x1, Pallas kernels, fused_body(): pl.pallas_call(functools.partial(fused, n_sx), out_shape=(jax.ShapeDtypeS...  83.3 us
    unnamed x5, local copies, waits for them, and re-layouts  8.26 us

profile of v1, /device:TPU:19, one launch (start us, length us, event | category | flops | bytes accessed | tf_op | source)
XLA Modules:
  0.0 92.2 jit_solution(6353165125960161779)
XLA Ops:
  0.6 83.3 %shard_map.92 = (bf16[256,256]{1,0:T(8,128)(2,1)}, bf16[2,32,32,128]{3,2,1,0:T(8,128)(2,1)}, f32[216,128]{1,0:T(8,128)}, f32[64,256]{1,0:T(8,128)}, f32[432,256]{1,0:T(8,128)}) custom-call(bf16[2,32,32,128]{3,2,1,0:T(8,128)(2,1)} %feat.1, bf16[3456,128]{1,0:T(8,128)(2,1)} %wu.1, bf16[1024,256]{1,0:T(8,128)(2,1)} %dw.1, bf16[6912,256]{1,0:T(8,128)(2,1)} %wl.1, ...), custom_call_target="tpu_custom_call" | custom-call | flops 8999999488 | bytes 12000000 | tf_op jit(solution)/shard_map/pallas_call | solution.py:582
  84.0 1.6 %copy.15 = bf16[1,16,16,256]{3,2,1,0:T(8,128)(2,1)} copy(bf16[1,16,16,256]{3,2,1,0:T(8,128)(2,1)} %bitcast.2) | data formatting | bytes 262144
  85.5 1.9 %copy.16 = bf16[2,32,32,128]{3,2,1,0:T(8,128)(2,1)} copy(bf16[2,32,32,128]{3,2,1,0:T(8,128)(2,1)} %get-tuple-element.21) | data formatting | bytes 1048576
  87.4 1.5 %copy.17 = f32[216,128]{1,0:T(8,128)} copy(f32[216,128]{1,0:T(8,128)} %get-tuple-element.22) | data formatting | bytes 221184
  88.9 1.5 %copy.18 = f32[64,256]{1,0:T(8,128)} copy(f32[64,256]{1,0:T(8,128)} %get-tuple-element.23) | data formatting | bytes 131072
  90.4 1.8 %copy.19 = f32[432,256]{1,0:T(8,128)} copy(f32[432,256]{1,0:T(8,128)} %get-tuple-element.24) | data formatting | bytes 884736

commit v2 on v1

--- a/solution.py
+++ b/solution.py
@@ -216,9 +216,9 @@
 
 def fused(n_sx, feat, wu, dw, wl, cot, bott, gfeat, gup, gdown, glow,
           fx, gx, hx, cx, call, ht, htr, xz, gz, hz, cz, wf, wb, wlf, wlb, wd, wtl, su, sd,
-          pu, hu, gzt, hcat, ghl, pl_low, hp, at, gl, s1, r1, s2, r2,
+          pu, hu, gzt, hcat, ghl, pl_low, hp, at, gl, s1, r1, s2, ry, s3, r2,
           f_s, f_r, g_s, g_r, h_s, h_r, c_s, c_r, ca_s, ca_r, cf_s, cf_r, t_s, t_r,
-          a_s, a_r, b_s, b_r):
+          a_s, a_r, b_s, b_r, y_s, y_r, m_s, m_r):
     g, i, j = lax.axis_index("groups"), lax.axis_index("sx"), lax.axis_index("sy")
     k = 1 - j
     me = 2 * i + j
@@ -307,6 +307,47 @@
     c_start, c_wait, c_done = halo(cx, 1, 16, c_s, c_r)
     c_start()
     f_start()
+
+    nz = n_sx // 2
+    zc, yc = i // 2, i % 2
+    mate = i + 1 - 2 * yc
+    part_copy = remote(call.at[me], call.at[me], y_s, y_r, (g, mate, j))
+    part_copy.start()
+
+    def hop(way, step, p):
+        src = zc - step if way == 0 else zc + step
+        inside = src >= 0 if way == 0 else src < nz
+        more = zc < nz - 1 if way == 0 else zc > 0
+        blk = call.at[2 * (2 * jnp.clip(src, 0, nz - 1) + p) + j]
+        to = jnp.clip(i + 2 if way == 0 else i - 2, 0, n_sx - 1)
+        slot = way * n_sx + step * 2 + p
+        return inside & more, inside, remote(blk, blk, ca_s.at[slot], ca_r.at[slot], (g, to, j))
+
+    def landed(way, step, p):
+        src = zc - step if way == 0 else zc + step
+        inside = src >= 0 if way == 0 else src < nz
+        blk = call.at[2 * (2 * jnp.clip(src, 0, nz - 1) + p) + j]
+        slot = way * n_sx + (step - 1) * 2 + p
+        return inside, remote(blk, blk, ca_s.at[slot], ca_r.at[slot], (g, i, k))
+
+    def chain(step):
+        for way in range(2):
+            for p in range(2):
+                if step:
+                    inside, got = landed(way, step, p)
+                    guard(inside, got.wait_recv)
+                if step < nz - 1:
+                    go, _, copy = hop(way, step, p)
+                    guard(go, copy.start)
+
+    def forward_copy(q):
+        blk = call.at[2 * q + j]
+        return remote(blk, blk, cf_s.at[q], cf_r.at[q], (g, i, k))
+
+    def forward_recv(q):
+        blk = call.at[2 * q + k]
+        return remote(blk, blk, cf_s.at[q], cf_r.at[q], (g, i, k))
+
     edges(fx, 2, 32)
     edges(gx, 2, 32)
     edges(hx, 1, 16)
@@ -356,28 +397,8 @@
 
     f_wait()
 
-    def gather_copy(q):
-        to = lax.rem(i + q, n_sx)
-        return remote(call.at[me], call.at[me], ca_s.at[q], ca_r.at[q], (g, to, j))
-
-    def gather_recv(q):
-        frm = lax.rem(i - q + n_sx, n_sx)
-        blk = call.at[2 * frm + j]
-        return remote(blk, blk, ca_s.at[q], ca_r.at[q], (g, i, k))
-
-    def forward_copy(q):
-        frm = lax.rem(i - q + n_sx, n_sx)
-        blk = call.at[2 * frm + j]
-        return remote(blk, blk, cf_s.at[q], cf_r.at[q], (g, i, k))
-
-    def forward_recv(q):
-        frm = lax.rem(i - q + n_sx, n_sx)
-        blk = call.at[2 * frm + k]
-        return remote(blk, blk, cf_s.at[q], cf_r.at[q], (g, i, k))
-
-    for q in range(1, n_sx):
-        gather_copy(q).start()
-    forward_copy(0).start()
+    part_copy.wait_recv()
+    chain(0)
 
     def upper_taps(src, dst, s, y0, ny):
         parts = depth_taps(src[s, pl.ds(y0, ny)].reshape(ny * 32, 128), 32)
@@ -440,6 +461,7 @@
         return 0
     lax.fori_loop(0, 8, grad_pre, 0)
     g_start()
+    chain(1)
 
     for s in range(2):
         upper_taps(gx, gz, s + 1, 1, 32)
@@ -478,17 +500,10 @@
 
     pair.wait_recv()
     for q in range(n_sx):
-        s2[q] = (s1[j, q].astype(F32) + r1[q].astype(F32)).astype(BF)
-
-    def sum_copy(q):
-        to = lax.rem(i + q, n_sx)
-        return remote(s2.at[to], r2.at[q], b_s.at[q], b_r.at[q], (g, to, j))
-    for q in range(1, n_sx):
-        sum_copy(q).start()
-
-    for q in range(1, n_sx):
-        gather_recv(q).wait_recv()
-        forward_copy(q).start()
+        s2[q % 2, q // 2] = (s1[j, q].astype(F32) + r1[q].astype(F32)).astype(BF)
+    mate_copy = remote(s2.at[1 - yc], ry, m_s, m_r, (g, mate, j))
+    mate_copy.start()
+    chain(2)
 
     g_wait()
     upper_taps(gx, gz, 0, 0, 34)
@@ -506,6 +521,19 @@
         gfeat[s, pl.ds(y0, 16)] = acc.astype(BF).reshape(16, 32, 128)
         return 0
     lax.fori_loop(0, 4, conv_down, 0)
+
+    mate_copy.wait_recv()
+    for q in range(nz):
+        s3[q] = (s2[yc, q].astype(F32) + ry[q].astype(F32)).astype(BF)
+
+    def sum_copy(q):
+        to = lax.rem(zc + q, nz)
+        return remote(s3.at[to], r2.at[q], b_s.at[q], b_r.at[q], (g, 2 * to + yc, j))
+    for q in range(1, nz):
+        sum_copy(q).start()
+    chain(3)
+    for q in range(n_sx):
+        forward_copy(q).start()
 
     for q in range(1, total):
         turn_recv(q).wait_recv()
@@ -534,8 +562,8 @@
     for h in range(2):
         glow[:, h * 128:(h + 1) * 128] = gl[h]
 
-    rows = s2[i].astype(F32)
-    for q in range(1, n_sx):
+    rows = s3[zc].astype(F32)
+    for q in range(1, nz):
         blk = r2.at[q]
         remote(blk, blk, b_s.at[q], b_r.at[q], (g, i, k)).wait_recv()
         rows += r2[q].astype(F32)
@@ -548,13 +576,28 @@
     h_done()
     c_done()
     pair.wait_send()
-    for q in range(1, n_sx):
-        gather_copy(q).wait_send()
+    part_copy.wait_send()
+    mate_copy.wait_send()
+    for q in range(1, nz):
         sum_copy(q).wait_send()
+    for way in range(2):
+        for step in range(nz - 1):
+            for p in range(2):
+                go, _, copy = hop(way, step, p)
+                guard(go, copy.wait_send)
     for q in range(n_sx):
         forward_copy(q).wait_send()
     for q in range(1, total):
         turn_copy(q).wait_send()
+
+
+def hand_on(*refs):
+    sems = refs[10]
+    copies = [pltpu.make_async_copy(refs[m], refs[5 + m], sems.at[m]) for m in range(5)]
+    for copy in copies:
+        copy.start()
+    for copy in copies:
+        copy.wait()
 
 
 def fused_body(feature, weight_upper, down_weight_matrix, weight_lower, cotangent):
@@ -572,11 +615,11 @@
         V((2, 32, 32, 128), F32), V((2, 16, 2, 32, 128), F32), V((384, 2048), BF),
         V((256, 1024), BF), V((256, 256), F32), V((256, 256), BF),
         V((16, 5376), F32), V((432, 4096), BF), V((2, 432, 128), F32),
-        V((2, n_sx, 352, 128), BF), V((n_sx, 352, 128), BF), V((n_sx, 352, 128), BF),
-        V((n_sx, 352, 128), BF),
+        V((2, n_sx, 352, 128), BF), V((n_sx, 352, 128), BF), V((2, n_sx // 2, 352, 128), BF),
+        V((n_sx // 2, 352, 128), BF), V((n_sx // 2, 352, 128), BF), V((n_sx // 2, 352, 128), BF),
         S((5,)), S((5,)), S((5,)), S((5,)), S((5,)), S((5,)), S((5,)), S((5,)),
-        S((n_sx,)), S((n_sx,)), S((n_sx,)), S((n_sx,)), S((total,)), S((total,)),
-        S, S, S((n_sx,)), S((n_sx,)),
+        S((2 * n_sx,)), S((2 * n_sx,)), S((n_sx,)), S((n_sx,)), S((total,)), S((total,)),
+        S, S, S((n_sx,)), S((n_sx,)), S, S, S, S,
     ]
     vm = pl.BlockSpec(memory_space=pltpu.VMEM)
     bott, gfeat, gup, gdown, glow = pl.pallas_call(
@@ -596,6 +639,15 @@
         cost_estimate=pl.CostEstimate(flops=9_000_000_000, bytes_accessed=12_000_000,
                                       transcendentals=600_000),
     )(feature, weight_upper, down_weight_matrix, weight_lower, cotangent.reshape(256, 256))
+    results = (bott, gfeat, gup, gdown, glow)
+    anywhere = pl.BlockSpec(memory_space=pl.ANY)
+    bott, gfeat, gup, gdown, glow = pl.pallas_call(
+        hand_on,
+        out_shape=tuple(jax.ShapeDtypeStruct(r.shape, r.dtype) for r in results),
+        in_specs=[anywhere] * 5,
+        out_specs=(anywhere,) * 5,
+        scratch_shapes=[S((5,))],
+    )(*results)
     return (bott.reshape(1, 16, 16, 256), gfeat, gup, gdown, glow)
 
 

time: 92.5 us -> 113 us (1.22)
  the two profiles are of different devices: /device:TPU:19 before, /device:TPU:0 now
where the time goes in v2:
time: 113 us; the launch traced here: 112 us
  Pallas kernels  112 us (99%)
    pallas_call x1, Pallas kernels, fused_body(): pl.pallas_call(functools.partial(fused, n_sx), out_shape=(jax.ShapeDtypeS...  72.1 us
    pallas_call x1, Pallas kernels, fused_body(): pl.pallas_call(hand_on, out_shape=tuple((jax.ShapeDtypeStruct(r.shape, r....  39.7 us

profile of v2, /device:TPU:0, one launch (start us, length us, event | category | flops | bytes accessed | tf_op | source)
XLA Modules:
  0.0 112.5 jit_solution(8432961221817474746)
XLA Ops:
  0.6 72.1 %shard_map.92 = (bf16[256,256]{1,0:T(8,128)(2,1)}, bf16[2,32,32,128]{3,2,1,0:T(8,128)(2,1)}, f32[216,128]{1,0:T(8,128)}, f32[64,256]{1,0:T(8,128)}, f32[432,256]{1,0:T(8,128)}) custom-call(bf16[2,32,32,128]{3,2,1,0:T(8,128)(2,1)} %feat.1, bf16[3456,128]{1,0:T(8,128)(2,1)} %wu.1, bf16[1024,256]{1,0:T(8,128)(2,1)} %dw.1, bf16[6912,256]{1,0:T(8,128)(2,1)} %wl.1, ...), custom_call_target="tpu_custom_call" | custom-call | flops 8999999488 | bytes 12000000 | tf_op jit(solution)/shard_map/pallas_call | solution.py:625
  72.7 39.7 %shard_map.93 = (bf16[256,256]{1,0:T(8,128)(2,1)}, bf16[2,32,32,128]{3,2,1,0:T(8,128)(2,1)}, f32[216,128]{1,0:T(8,128)}, f32[64,256]{1,0:T(8,128)}, f32[432,256]{1,0:T(8,128)}) custom-call(bf16[256,256]{1,0:T(8,128)(2,1)} %get-tuple-element.15.refs_0_, bf16[2,32,32,128]{3,2,1,0:T(8,128)(2,1)} %get-tuple-element.16.refs_1_, ...), custom_call_target="tpu_custom_call" | custom-call | tf_op jit(solution)/shard_map/pallas_call | solution.py:644
